TPU v7x, 256 devices: a whole 4x4x8 slice. The times are simulated.
256 devices in a mesh: row: 16 (over z, x_hi), col: 16 (over x_lo, y, core).
Axes of the slice: x: 4 (x_hi: 2, x_lo: 2; x = x_hi * 2 + x_lo), y: 4, z: 8, core: 2. Of those that a mesh axis runs over, the one named last changes fastest.
Arguments:
- activations: bfloat16 [2048, 12288], P('row', 'col'), may hold values from -6 to 6
- out_grad: bfloat16 [2048, 12288], P('row', 'col'), may hold values from -6 to 6
- pre_act: bfloat16 [2048, 24576], P('col', 'row'), may hold values from -8 to 8
- w_in: bfloat16 [12288, 24576], P('col', 'row'), may hold values from -0.0546875 to 0.0546875
- w_out: bfloat16 [24576, 12288], P('row', 'col'), may hold values from -0.0390625 to 0.0390625
Outputs:
- grad_input: bfloat16 [2048, 12288], P('row', 'col')
- grad_w_in: bfloat16 [12288, 24576], P('col', 'row')
All inputs are finite; a program needn't handle non-finite values.
Results may differ from a plain program's by a relative error of at most 0.04.
Values may be sent and summed in bfloat16 or wider, within the bound.
No kernel may reach another device: no remote copies, remote signals or barrier semaphores. Data moves between devices by JAX's collectives and lax.ppermute only.
A program may use at most 64 MiB of HBM per device.

v0:
```python
import math

import jax
import jax.numpy as jnp
from jax import lax
from jax.sharding import PartitionSpec as P


def gelu_slope(hidden):
    coeff = math.sqrt(2.0 / math.pi)
    inner = coeff * (hidden + 0.044715 * hidden * hidden * hidden)
    tanh_val = jnp.tanh(inner)
    return 0.5 * (1.0 + tanh_val) + 0.5 * hidden * (1.0 - tanh_val * tanh_val) * coeff * (
        1.0 + 3.0 * 0.044715 * hidden * hidden
    )


def times_trans(left, right):
    return lax.dot_general(
        left, right, (((1,), (1,)), ((), ())), preferred_element_type=jnp.float32
    )


def trans_times(left, right):
    return lax.dot_general(
        left, right, (((0,), (0,)), ((), ())), preferred_element_type=jnp.float32
    )


def local(activations, out_grad, pre_act, w_in, w_out):
    act_cols, grad_cols = (
        lax.all_gather(activations, "row", axis=0, tiled=True),
        lax.all_gather(out_grad, "row", axis=0, tiled=True),
    )
    rows_here = grad_cols
    grad_act = lax.psum_scatter(
        times_trans(rows_here, w_out).astype(jnp.bfloat16), "col", scatter_dimension=0, tiled=True
    ).astype(jnp.float32)
    hidden_grad = (grad_act * gelu_slope(pre_act.astype(jnp.float32))).astype(jnp.bfloat16)
    hidden_full = lax.all_gather(hidden_grad, "col", axis=0, tiled=True)
    rows_here = hidden_full
    grad_input = lax.psum_scatter(
        times_trans(rows_here, w_in).astype(jnp.bfloat16), "row", scatter_dimension=0, tiled=True
    )
    grad_w_in = trans_times(act_cols, hidden_full).astype(jnp.bfloat16)
    return (grad_input, grad_w_in)


def solution(mesh):
    in_specs = (P("row", "col"), P("row", "col"), P("col", "row"), P("col", "row"), P("row", "col"))
    out_specs = (P("row", "col"), P("col", "row"))
    return jax.shard_map(local, mesh=mesh, in_specs=in_specs, out_specs=out_specs, check_vma=False)
```

profile of v0, /device:TPU:8, one launch (start us, length us, event | category | flops | bytes accessed | tf_op | source)
XLA Modules:
  0.0 545.9 jit_solution(9215376884248948251)
XLA Ops:
  7.2 0.0 copy-start
  7.2 0.0 all-gather.4.cloned.1.call-start
  7.2 0.7 all-gather.4.cloned.1.call-update
  7.9 0.0 reduce-scatter.3.cloned.1.call-start
  8.0 98.9 %all-gather.4.cloned.1.call-done = bf16[2048,768]{1,0:T(8,128)(2,1)} async-done(((bf16[128,768]{1,0:T(8,128)(2,1)}), bf16[2048,768]{1,0:T(8,128)(2,1)}) %all-gather.4.cloned.1.call-update) | async-done | bytes 3145744 | tf_op jit(solution)/shard_map/all_gather | solution.py:33
  106.8 0.0 copy-done
  106.8 8.9 %convolution_convert_fusion = bf16[2048,1536]{1,0:T(8,128)(2,1)} fusion(bf16[2048,768]{1,0:T(8,128)(2,1)} %all-gather.4.cloned.1.call-done, bf16[1536,768]{1,0:T(8,128)(2,1)S(1)} %copy-done), kind=kOutput, calls=%fused_computation | convolution fusion | flops 4834983936 | bytes 11796480 | tf_op jit(solution)/shard_map/dot_general | solution.py:19
  115.7 0.0 copy-start.1
  115.7 0.0 reduce-scatter.3.cloned.1.call-update
  115.7 0.0 all-gather.6.cloned.1.call-start
  115.8 65.7 %reduce-scatter.3.cloned.1.call-done = bf16[128,1536]{1,0:T(8,128)(2,1)} async-done(((bf16[2048,1536]{1,0:T(8,128)(2,1)}), bf16[128,1536]{1,0:T(8,128)(2,1)}) %reduce-scatter.3.cloned.1.call-update) | async-done | bytes 393232 | tf_op jit(solution)/shard_map/reduce_scatter | solution.py:36
  181.5 0.0 copy-done.1
  181.5 2.3 fusion.8
  183.8 0.0 all-gather.6.cloned.1.call-update
  183.8 0.0 all-gather.8.cloned.1.call-start
  183.9 0.5 all-gather.8.cloned.1.call-update
  184.4 0.0 reduce-scatter.5.cloned.1.call-start
  184.4 47.2 %all-gather.6.cloned.1.call-done = bf16[2048,1536]{1,0:T(8,128)(2,1)} async-done(((bf16[128,1536]{1,0:T(8,128)(2,1)}), bf16[2048,1536]{1,0:T(8,128)(2,1)}) %all-gather.6.cloned.1.call-update) | async-done | bytes 6291472 | tf_op jit(solution)/shard_map/all_gather | solution.py:40
  231.6 9.1 %convolution_convert_fusion.2 = bf16[2048,768]{1,0:T(8,128)(2,1)} fusion(bf16[2048,1536]{1,0:T(8,128)(2,1)} %all-gather.6.cloned.1.call-done, bf16[768,1536]{1,0:T(8,128)(2,1)} %param.8), kind=kOutput, calls=%fused_computation.2 | convolution fusion | flops 4833411072 | bytes 11796480 | tf_op jit(solution)/shard_map/dot_general | solution.py:19
  240.7 0.0 reduce-scatter.5.cloned.1.call-update
  240.8 87.6 %all-gather.8.cloned.1.call-done = bf16[2048,768]{1,0:T(8,128)(2,1)} async-done(((bf16[128,768]{1,0:T(8,128)(2,1)}), bf16[2048,768]{1,0:T(8,128)(2,1)}) %all-gather.8.cloned.1.call-update) | async-done | bytes 3145744 | tf_op jit(solution)/shard_map/all_gather | solution.py:32
  328.4 9.2 %fusion = bf16[768,1536]{0,1:T(8,128)(2,1)} fusion(bf16[2048,1536]{1,0:T(8,128)(2,1)} %all-gather.6.cloned.1.call-done, bf16[2048,768]{1,0:T(8,128)(2,1)} %all-gather.8.cloned.1.call-done), kind=kOutput, calls=%fused_computation.3 | convolution fusion | flops 4833017856 | bytes 11796480 | tf_op jit(solution)/shard_map/dot_general | solution.py:25
  337.6 4.3 copy.7
  341.9 197.5 %reduce-scatter.5.cloned.1.call-done = bf16[128,768]{1,0:T(8,128)(2,1)} async-done(((bf16[2048,768]{1,0:T(8,128)(2,1)}), bf16[128,768]{1,0:T(8,128)(2,1)}) %reduce-scatter.5.cloned.1.call-update) | async-done | bytes 196624 | tf_op jit(solution)/shard_map/reduce_scatter | solution.py:42
Async XLA Ops:
  7.2 99.7 %copy-start = (bf16[1536,768]{1,0:T(8,128)(2,1)S(1)}, bf16[1536,768]{1,0:T(8,128)(2,1)}, u32[]{:S(2)}) copy-start(bf16[1536,768]{1,0:T(8,128)(2,1)} %param.9) | copy-start | bytes 7077892
  7.2 99.6 %all-gather.4.cloned.1.call-start = ((), (), s32[]{:S(2)}) async-start(), calls=%async_computation.2 | async-start | bytes 3342336 | tf_op jit(solution)/shard_map/all_gather | solution.py:33
  7.9 173.6 %reduce-scatter.3.cloned.1.call-start = ((), (), s32[]{:S(2)}) async-start(), calls=%async_computation.3 | async-start | bytes 6684672 | tf_op jit(solution)/shard_map/reduce_scatter | solution.py:36
  115.7 65.8 %copy-start.1 = (bf16[128,1536]{1,0:T(8,128)(2,1)S(1)}, bf16[128,1536]{1,0:T(8,128)(2,1)}, u32[]{:S(2)}) copy-start(bf16[128,1536]{1,0:T(8,128)(2,1)} %param.7) | copy-start | bytes 1179652
  115.7 115.8 %all-gather.6.cloned.1.call-start = ((), (), s32[]{:S(2)}) async-start(), calls=%async_computation.4 | async-start | bytes 6684672 | tf_op jit(solution)/shard_map/all_gather | solution.py:40
  183.8 144.6 %all-gather.8.cloned.1.call-start = ((), (), s32[]{:S(2)}) async-start(), calls=%async_computation.6 | async-start | bytes 3342336 | tf_op jit(solution)/shard_map/all_gather | solution.py:32
  184.4 355.0 %reduce-scatter.5.cloned.1.call-start = ((), (), s32[]{:S(2)}) async-start(), calls=%async_computation.5 | async-start | bytes 3342336 | tf_op jit(solution)/shard_map/reduce_scatter | solution.py:42
Sparse Core Ops, SparseCore 0:
  10.6 96.1 all-gather.3
  115.9 65.5 reduce-scatter.2
  183.9 47.6 all-gather.5
  234.0 94.2 all-gather.7
  332.8 206.5 reduce-scatter.4
where the time goes:
time: 546 us
  waiting for transfers between devices  498 us (91%)
  matrix products  27.3 us (5%)
  between operations  13.8 us (3%)
    reduce_scatter x1, waiting for transfers between devices, local(): lax.psum_scatter(times_trans(rows_here, w_in).astype(jnp.bfloat16), 'row'...  198 us
    all_gather x1, waiting for transfers between devices, local(): lax.all_gather(out_grad, 'row', axis=0, tiled=True)  98.9 us
    all_gather x1, waiting for transfers between devices, local(): lax.all_gather(activations, 'row', axis=0, tiled=True)  87.6 us
    reduce_scatter x1, waiting for transfers between devices, local(): lax.psum_scatter(times_trans(rows_here, w_out).astype(jnp.bfloat16), 'col...  65.7 us
    all_gather x1, waiting for transfers between devices, local(): hidden_full = lax.all_gather(hidden_grad, 'col', axis=0, tiled=True)  47.2 us
    dot_general x2, matrix products, times_trans(): lax.dot_general(left, right, (((1,), (1,)), ((), ())), preferred_element_...  18 us
  transfers between devices with their start and end apart: 5, of which 5 were waited for; matrix products, arithmetic and copies ran while one was open for 4% of the time, Pallas kernels for 0%

commit v1 on v0

v1 whole, which is shorter than its diff:
```python
import math

import jax
import jax.numpy as jnp
from jax import lax
from jax.sharding import PartitionSpec as P

NZ, NH, NL, NY, NC = 8, 2, 2, 4, 2
TOK = 128
SUB = 8
CHUNKS = ((0, 1, -1), (2, -2, 3, -3, 4))


def gelu_slope(hidden):
    coeff = math.sqrt(2.0 / math.pi)
    inner = coeff * (hidden + 0.044715 * hidden * hidden * hidden)
    tanh_val = jnp.tanh(inner)
    return 0.5 * (1.0 + tanh_val) + 0.5 * hidden * (1.0 - tanh_val * tanh_val) * coeff * (
        1.0 + 3.0 * 0.044715 * hidden * hidden
    )


def times_trans(left, right):
    return lax.dot_general(
        left, right, (((left.ndim - 1,), (1,)), ((), ())), preferred_element_type=jnp.float32
    )


def trans_times(left, right):
    return lax.dot_general(
        left, right, (((0,), (0,)), ((), ())), preferred_element_type=jnp.float32
    )


def f32(x):
    return x.astype(jnp.float32)


def bf16(x):
    return x.astype(jnp.bfloat16)


def send_z(x, step):
    pairs = [
        (z * NH + h, (z + step) % NZ * NH + h) for z in range(NZ) for h in range(NH)
    ]
    return lax.ppermute(x, "row", pairs)


def swap_h(x):
    return lax.ppermute(x, "row", [(r, r ^ 1) for r in range(NZ * NH)])


def send_y(x, step):
    pairs = [
        ((l * NY + y) * NC + c, (l * NY + (y + step) % NY) * NC + c)
        for l in range(NL)
        for y in range(NY)
        for c in range(NC)
    ]
    return lax.ppermute(x, "col", pairs)


def swap_l(x):
    return lax.ppermute(x, "col", [(j, j ^ (NY * NC)) for j in range(NL * NY * NC)])


def swap_c(x):
    return lax.ppermute(x, "col", [(j, j ^ 1) for j in range(NL * NY * NC)])


def roll_to(x, start):
    twice = jnp.concatenate([x, x], axis=0)
    return lax.dynamic_slice_in_dim(twice, start, x.shape[0], axis=0)


def flip_if(x, flag, axis):
    return jnp.where(flag == 1, jnp.flip(x, axis), x)


def to_relative(x, l, y, c):
    x = x.reshape(NL, NY, NC, SUB, -1)
    x = flip_if(flip_if(x, l, 0), c, 2)
    x = roll_to(x.transpose(1, 2, 0, 3, 4), y)
    return x.transpose(1, 2, 0, 3, 4).reshape(TOK, -1)


def from_relative(x, l, y, c):
    x = x.reshape(NC, NL, NY, SUB, -1).transpose(2, 0, 1, 3, 4)
    x = roll_to(x, (NY - y) % NY).transpose(2, 0, 1, 3, 4)
    return flip_if(flip_if(x, l, 0), c, 2).reshape(TOK, -1)


def local(activations, out_grad, pre_act, w_in, w_out):
    row, col = lax.axis_index("row"), lax.axis_index("col")
    z, h = row // NH, row % NH
    l, y, c = col // (NY * NC), col // NC % NY, col % NC
    width, hid = activations.shape[1], w_in.shape[1]

    own = {0: to_relative(out_grad, l, y, c)}
    for step in (1, 2, 3):
        own[-step] = send_z(own[1 - step], 1)
        own[step] = send_z(own[step - 1], -1)
    half = TOK // 2
    own[4] = jnp.concatenate([send_z(own[-3][:half], 1), send_z(own[3][half:], -1)], axis=0)
    other = {}
    for group in ((0,), (1, -1), (2, -2), (3, -3), (4,)):
        got = swap_h(jnp.stack([own[d] for d in group]))
        for at, d in enumerate(group):
            other[d] = got[at]

    act = to_relative(activations, l, y, c)
    act = jnp.concatenate([act, swap_h(act)], axis=0)
    groups = [[zz * NH + hh for zz in range(NZ)] for hh in range(NH)]
    act_all = lax.all_gather(act, "row", axis_index_groups=groups, axis=0, tiled=True)
    act_all = act_all.reshape(NZ, NH * TOK, width)

    pre = lax.all_to_all(pre_act, "col", split_axis=0, concat_axis=0, tiled=True)
    pre = roll_to(pre.reshape(NZ, NH, SUB, hid), z)
    pre = flip_if(pre, h, 1)

    w_grad = None
    share = {}
    for chunk in CHUNKS:
        n = NH * len(chunk)
        x = jnp.stack([v[d] for d in chunk for v in (own, other)])
        x = x.reshape(n, NC, NL * NY * SUB, width)
        away = bf16(times_trans(x[:, 1], w_out))
        away = swap_c(away)
        part = bf16(times_trans(x[:, 0], w_out) + f32(away)).reshape(n, NL, NY, SUB, hid)
        total = f32(part[:, :, 0])
        for step in (2, 1, 3):
            total = total + f32(send_y(part[:, :, step], step))
        total = bf16(total)
        grad_act = f32(total[:, 0]) + f32(swap_l(total[:, 1]))
        slope = gelu_slope(f32(jnp.concatenate([pre[d % NZ] for d in chunk], axis=0)))
        hidden = bf16(grad_act * slope)

        pair = jnp.stack([hidden, swap_l(hidden)], axis=1)
        whole = [pair] + [send_y(pair, step) for step in (3, 2, 1)]
        whole = jnp.stack(whole, axis=2)
        whole = jnp.stack([whole, swap_c(whole)], axis=1).reshape(n * TOK, hid)

        x_grad = bf16(times_trans(whole, w_in)).reshape(len(chunk), NH, TOK, width)
        got = swap_h(x_grad[:, 1])
        for at, d in enumerate(chunk):
            share[d] = f32(x_grad[at, 0]) + f32(got[at])

        act_here = jnp.concatenate(
            [lax.dynamic_index_in_dim(act_all, (z + d) % NZ, 0, keepdims=False) for d in chunk], axis=0
        )
        term = trans_times(act_here, whole)
        w_grad = term if w_grad is None else w_grad + term

    up = send_z(bf16(share[4][:half]), 1)
    down = send_z(bf16(share[4][half:]), -1)
    rest = jnp.zeros((half, width), jnp.float32)
    up = f32(jnp.concatenate([up, bf16(rest)], axis=0))
    down = f32(jnp.concatenate([bf16(rest), down], axis=0))
    for d in (3, 2, 1):
        up = f32(send_z(bf16(share[d] + up), 1))
        down = f32(send_z(bf16(share[-d] + down), -1))
    grad_input = from_relative(bf16(share[0] + up + down), l, y, c)
    return (grad_input, bf16(w_grad))


def solution(mesh):
    in_specs = (P("row", "col"), P("row", "col"), P("col", "row"), P("col", "row"), P("row", "col"))
    out_specs = (P("row", "col"), P("col", "row"))
    return jax.shard_map(local, mesh=mesh, in_specs=in_specs, out_specs=out_specs, check_vma=False)
```

time: 546 us -> 315 us (0.58); the launches traced: 546 us -> 309 us
  waiting for transfers between devices: 498 us -> 170 us
  starting transfers between devices: 0.2 us -> 83.2 us
  local copies, waits for them, and re-layouts: 4.28 us -> 17.1 us
  matrix products: 27.3 us -> 17.7 us
    reduce_scatter x2 -> x0, waiting for transfers between devices: 263 us -> none  [the longest x1 198 us: local(): lax.psum_scatter(times_trans(rows_here, w_in).astype(jnp.bfloat16), 'row'...]
    all_gather x3 -> x1, waiting for transfers between devices: 234 us -> 42.9 us  [local(): lax.all_gather(act, 'row', axis_index_groups=groups, axis=0, tiled=True)]
    ppermute x0 -> x44, waiting for transfers between devices: none -> 127 us  [the longest x12 43 us: send_y(): return lax.ppermute(x, 'col', pairs)]
    ppermute x0 -> x44, starting transfers between devices: none -> 77.3 us  [the longest x16 28.4 us: send_z(): return lax.ppermute(x, 'row', pairs)]
    dot_general x2 -> x6, matrix products: 18 us -> 11 us  [times_trans(): lax.dot_general(left, right, (((left.ndim - 1,), (1,)), ((), ())), prefer...]
    unnamed x5 -> x47, local copies, waits for them, and re-layouts: 4.28 us -> 10.7 us
    all_to_all x0 -> x1, starting transfers between devices: none -> 5.86 us  [local(): lax.all_to_all(pre_act, 'col', split_axis=0, concat_axis=0, tiled=True)]
  transfers between devices with their start and end apart: 5 -> 46, of which waited for: 5 -> 25; matrix products, arithmetic and copies ran while one was open for 4% -> 7% of each run, Pallas kernels for 0% -> 0%
where the time goes in v1:
time: 315 us; the launch traced here: 309 us
  waiting for transfers between devices  170 us (54%)
  starting transfers between devices  83.2 us (26%)
  matrix products  17.7 us (6%)
  local copies, waits for them, and re-layouts  17.1 us (5%)
  between operations  15.2 us (5%)
  other arithmetic  6.14 us (2%)
    ppermute x12, waiting for transfers between devices, send_y(): return lax.ppermute(x, 'col', pairs)  43 us
    all_gather x1, waiting for transfers between devices, local(): lax.all_gather(act, 'row', axis_index_groups=groups, axis=0, tiled=True)  42.9 us
    ppermute x8, waiting for transfers between devices, swap_h(): return lax.ppermute(x, 'row', [(r, r ^ 1) for r in range(NZ * NH)])  39.5 us
    ppermute x16, starting transfers between devices, send_z(): return lax.ppermute(x, 'row', pairs)  28.4 us
    ppermute x4, waiting for transfers between devices, swap_l(): lax.ppermute(x, 'col', [(j, j ^ NY * NC) for j in range(NL * NY * NC)])  21 us
    ppermute x16, waiting for transfers between devices, send_z(): return lax.ppermute(x, 'row', pairs)  20.3 us
    ppermute x12, starting transfers between devices, send_y(): return lax.ppermute(x, 'col', pairs)  18.1 us
    ppermute x8, starting transfers between devices, swap_h(): return lax.ppermute(x, 'row', [(r, r ^ 1) for r in range(NZ * NH)])  16.6 us
  transfers between devices with their start and end apart: 46, of which 25 were waited for; matrix products, arithmetic and copies ran while one was open for 7% of the time, Pallas kernels for 0%

profile of v1, /device:TPU:8, one launch (start us, length us, event | category | flops | bytes accessed | tf_op | source)
XLA Modules:
  0.0 308.9 jit_solution(2695797075519976617)
XLA Ops:
  8.5 5.9 %collective-permute-start.1 = (bf16[128,768]{1,0:T(8,128)(2,1)S(1)}, bf16[128,768]{1,0:T(8,128)(2,1)S(1)}, u32[]{:S(2)}, u32[]{:S(2)}) collective-permute-start(bf16[128,768]{1,0:T(8,128)(2,1)S(1)} %bitcast.313), channel_id=1, source_target_pairs={{0,224},{16,240},{32,0},{48,16},{64,32},{80,48},{96,64},{112,80},{... | collective-permute-start | bytes 589832 | tf_op jit(solution)/shard_map/ppermute | solution.py:47
  14.5 5.9 %all-to-all-start = ((bf16[16,8,1536]{2,1,0:T(8,128)(2,1)}), bf16[16,8,1536]{2,1,0:T(8,128)(2,1)S(1)}, u32[]{:S(2)}, u32[]{:S(2)}) async-start(bf16[16,8,1536]{2,1,0:T(8,128)(2,1)} %bitcast.341), calls=%async_computation | async-start | bytes 786432 | tf_op jit(solution)/shard_map/all_to_all | solution.py:118
  28.7 4.5 %collective-permute-done = bf16[1,128,768]{2,1,0:T(8,128)(2,1)} collective-permute-done((bf16[1,128,768]{2,1,0:T(8,128)(2,1)S(1)}, bf16[1,128,768]{2,1,0:T(8,128)(2,1)}, u32[]{:S(2)}, u32[]{:S(2)}) %collective-permute-start) | collective-permute-done | bytes 196640 | tf_op jit(solution)/shard_map/ppermute | solution.py:51
  35.8 3.3 %collective-permute-start.18 = (bf16[128,768]{1,0:T(8,128)(2,1)}, bf16[128,768]{1,0:T(8,128)(2,1)S(1)}, u32[]{:S(2)}, u32[]{:S(2)}) collective-permute-start(bf16[128,768]{1,0:T(8,128)(2,1)} %collective-permute-done.15), channel_id=1, source_target_pairs={{0,224},{16,240},{32,0},{48,16},{64,32},{80,48},{96,64},{112,80},{... | collective-permute-start | bytes 589832 | tf_op jit(solution)/shard_map/ppermute | solution.py:47
  41.9 4.1 %collective-permute-done.19 = bf16[128,768]{1,0:T(8,128)(2,1)S(1)} collective-permute-done((bf16[128,768]{1,0:T(8,128)(2,1)S(1)}, bf16[128,768]{1,0:T(8,128)(2,1)S(1)}, u32[]{:S(2)}, u32[]{:S(2)}) %collective-permute-start.19) | collective-permute-done | bytes 196640 | tf_op jit(solution)/shard_map/ppermute | solution.py:47
  55.4 6.7 %collective-permute-done.20 = bf16[2,128,768]{2,1,0:T(8,128)(2,1)S(1)} collective-permute-done((bf16[2,128,768]{2,1,0:T(8,128)(2,1)S(1)}, bf16[2,128,768]{2,1,0:T(8,128)(2,1)S(1)}, u32[]{:S(2)}, u32[]{:S(2)}) %collective-permute-start.20) | collective-permute-done | bytes 393248 | tf_op jit(solution)/shard_map/ppermute | solution.py:51
  78.0 10.0 %collective-permute-done.25 = bf16[10,2,8,1536]{3,2,0,1:T(8,128)(2,1)S(1)} collective-permute-done((bf16[10,2,8,1536]{3,2,0,1:T(8,128)(2,1)S(1)}, bf16[10,2,8,1536]{3,2,0,1:T(8,128)(2,1)S(1)}, u32[]{:S(2)}, u32[]{:S(2)}) %collective-permute-start.25) | collective-permute-done | bytes 491552 | tf_op jit(solution)/shard_map/ppermute | solution.py:61
  88.0 9.7 %collective-permute-done.26 = bf16[10,2,8,1536]{3,2,0,1:T(8,128)(2,1)S(1)} collective-permute-done((bf16[10,2,8,1536]{3,2,0,1:T(8,128)(2,1)S(1)}, bf16[10,2,8,1536]{3,2,0,1:T(8,128)(2,1)S(1)}, u32[]{:S(2)}, u32[]{:S(2)}) %collective-permute-start.26) | collective-permute-done | bytes 491552 | tf_op jit(solution)/shard_map/ppermute | solution.py:61
  99.0 7.0 %collective-permute-done.28 = bf16[10,8,1536]{2,1,0:T(8,128)(2,1)S(1)} collective-permute-done((bf16[10,8,1536]{2,1,0:T(8,128)(2,1)S(1)}, bf16[10,8,1536]{2,1,0:T(8,128)(2,1)S(1)}, u32[]{:S(2)}, u32[]{:S(2)}) %collective-permute-start.28) | collective-permute-done | bytes 245792 | tf_op jit(solution)/shard_map/ppermute | solution.py:65
  108.4 5.0 %collective-permute-done.29 = bf16[10,8,1536]{2,1,0:T(8,128)(2,1)S(1)} collective-permute-done((bf16[10,8,1536]{2,1,0:T(8,128)(2,1)S(1)}, bf16[10,8,1536]{2,1,0:T(8,128)(2,1)S(1)}, u32[]{:S(2)}, u32[]{:S(2)}) %collective-permute-start.29) | collective-permute-done | bytes 245792 | tf_op jit(solution)/shard_map/ppermute | solution.py:65
  120.1 20.7 %collective-permute-done.30 = bf16[10,2,8,1536]{3,2,0,1:T(8,128)(2,1)S(1)} collective-permute-done((bf16[10,2,8,1536]{3,2,0,1:T(8,128)(2,1)S(1)}, bf16[10,2,8,1536]{3,2,0,1:T(8,128)(2,1)S(1)}, u32[]{:S(2)}, u32[]{:S(2)}) %collective-permute-start.30) | collective-permute-done | bytes 491552 | tf_op jit(solution)/shard_map/ppermute | solution.py:61
  142.6 9.0 %collective-permute-start.33 = (bf16[10,2,4,8,1536]{4,3,0,1,2:T(8,128)(2,1)S(1)}, bf16[10,2,4,8,1536]{4,3,0,1,2:T(8,128)(2,1)S(1)}, u32[]{:S(2)}, u32[]{:S(2)}) collective-permute-start(bf16[10,2,4,8,1536]{4,3,0,1,2:T(8,128)(2,1)S(1)} %get-tuple-element.8), channel_id=1, source_target_pairs={{0,1},{1,0},{2,3},{3,2},{4,5},{5,4},{6,7},{7,6},{8,9},{9,8},{10,11... | collective-permute-start | bytes 5898248 | tf_op jit(solution)/shard_map/ppermute | solution.py:69
  153.2 4.9 %collective-permute-done.8 = bf16[6,8,1536]{2,1,0:T(8,128)(2,1)S(1)} collective-permute-done((bf16[6,8,1536]{2,1,0:T(8,128)(2,1)S(1)}, bf16[6,8,1536]{2,1,0:T(8,128)(2,1)S(1)}, u32[]{:S(2)}, u32[]{:S(2)}) %collective-permute-start.8) | collective-permute-done | bytes 147488 | tf_op jit(solution)/shard_map/ppermute | solution.py:65
  159.7 4.1 %collective-permute-done.9 = bf16[6,8,1536]{2,1,0:T(8,128)(2,1)S(1)} collective-permute-done((bf16[6,8,1536]{2,1,0:T(8,128)(2,1)S(1)}, bf16[6,8,1536]{2,1,0:T(8,128)(2,1)S(1)}, u32[]{:S(2)}, u32[]{:S(2)}) %collective-permute-start.9) | collective-permute-done | bytes 147488 | tf_op jit(solution)/shard_map/ppermute | solution.py:65
  163.9 4.3 %collective-permute-start.10 = (bf16[6,2,8,1536]{3,2,1,0:T(8,128)(2,1)S(1)}, bf16[6,2,8,1536]{3,2,1,0:T(8,128)(2,1)S(1)}, u32[]{:S(2)}, u32[]{:S(2)}) collective-permute-start(bf16[6,2,8,1536]{3,2,1,0:T(8,128)(2,1)S(1)} %get-tuple-element.33), channel_id=1, source_target_pairs={{0,6},{1,7},{2,0},{3,1},{4,2},{5,3},{6,4},{7,5},{8,14},{9,15},{10,... | collective-permute-start | bytes 884744 | tf_op jit(solution)/shard_map/ppermute | solution.py:61
  180.9 18.0 %collective-permute-done.34 = bf16[5,128,768]{2,1,0:T(8,128)(2,1)S(1)} collective-permute-done((bf16[5,128,768]{2,1,0:T(8,128)(2,1)S(1)}, bf16[5,128,768]{2,1,0:T(8,128)(2,1)S(1)}, u32[]{:S(2)}, u32[]{:S(2)}) %collective-permute-start.34) | collective-permute-done | bytes 983072 | tf_op jit(solution)/shard_map/ppermute | solution.py:51
  207.1 4.8 %collective-permute-done.36 = bf16[128,768]{1,0:T(8,128)(2,1)S(1)} collective-permute-done((bf16[128,768]{1,0:T(8,128)(2,1)S(1)}, bf16[128,768]{1,0:T(8,128)(2,1)S(1)}, u32[]{:S(2)}, u32[]{:S(2)}) %collective-permute-start.36) | collective-permute-done | bytes 196640 | tf_op jit(solution)/shard_map/ppermute | solution.py:47
  214.0 3.8 %collective-permute-start.14 = (bf16[3,128,768]{2,1,0:T(8,128)(2,1)S(1)}, bf16[3,128,768]{2,1,0:T(8,128)(2,1)S(1)}, u32[]{:S(2)}, u32[]{:S(2)}) collective-permute-start(bf16[3,128,768]{2,1,0:T(8,128)(2,1)S(1)} %slice_bitcast_fusion.5), channel_id=1, source_target_pairs={{0,16},{16,0},{32,48},{48,32},{64,80},{80,64},{96,112},{112,96},{1... | collective-permute-start | bytes 1769480 | tf_op jit(solution)/shard_map/ppermute | solution.py:51
  219.3 3.8 %collective-permute-start.41 = (bf16[128,768]{1,0:T(8,128)(2,1)S(1)}, bf16[128,768]{1,0:T(8,128)(2,1)S(1)}, u32[]{:S(2)}, u32[]{:S(2)}) collective-permute-start(bf16[128,768]{1,0:T(8,128)(2,1)S(1)} %fusion.31), channel_id=1, source_target_pairs={{0,224},{16,240},{32,0},{48,16},{64,32},{80,48},{96,64},{112,80},{... | collective-permute-start | bytes 589832 | tf_op jit(solution)/shard_map/ppermute | solution.py:47
  227.9 3.8 %collective-permute-start.42 = (bf16[128,768]{1,0:T(8,128)(2,1)S(1)}, bf16[128,768]{1,0:T(8,128)(2,1)S(1)}, u32[]{:S(2)}, u32[]{:S(2)}) collective-permute-start(bf16[128,768]{1,0:T(8,128)(2,1)S(1)} %get-tuple-element.14), channel_id=1, source_target_pairs={{0,224},{16,240},{32,0},{48,16},{64,32},{80,48},{96,64},{112,80},{... | collective-permute-start | bytes 589832 | tf_op jit(solution)/shard_map/ppermute | solution.py:47
  231.7 3.5 %collective-permute-done.38 = bf16[128,768]{1,0:T(8,128)(2,1)S(1)} collective-permute-done((bf16[128,768]{1,0:T(8,128)(2,1)S(1)}, bf16[128,768]{1,0:T(8,128)(2,1)S(1)}, u32[]{:S(2)}, u32[]{:S(2)}) %collective-permute-start.38) | collective-permute-done | bytes 196640 | tf_op jit(solution)/shard_map/ppermute | solution.py:47
  237.3 5.6 %collective-permute-done.43 = bf16[128,768]{1,0:T(8,128)(2,1)S(1)} collective-permute-done((bf16[128,768]{1,0:T(8,128)(2,1)S(1)}, bf16[128,768]{1,0:T(8,128)(2,1)S(1)}, u32[]{:S(2)}, u32[]{:S(2)}) %collective-permute-start.43) | collective-permute-done | bytes 196640 | tf_op jit(solution)/shard_map/ppermute | solution.py:51
  244.7 42.9 %all-gather.2.cloned.1.call-done = bf16[2048,768]{1,0:T(8,128)(2,1)} async-done(((bf16[256,768]{1,0:T(8,128)(2,1)}), bf16[2048,768]{1,0:T(8,128)(2,1)}) %all-gather.2.cloned.1.call-update) | async-done | bytes 3145744 | tf_op jit(solution)/shard_map/all_gather | solution.py:115
  298.4 3.4 %add_convert_fusion = bf16[768,1536]{1,0:T(8,128)(2,1)} fusion(f32[768,1536]{1,0:T(8,128)S(1)} %fusion.70, bf16[768,1536]{1,0:T(8,128)(2,1)S(1)} %bitcast.294, bf16[256,768]{1,0:T(8,128)(2,1)S(1)} %get-tuple-element.3, bf16[256,768]{1,0:T(8,128)(2,1)S(1)} %get-tuple-element.4, bf16[256,768]{1,0:T(8,128)(2,1)S(1)} %get-tuple-element.2), kind=kOutput, calls=%fused_computation | convolution fusion | flops 1817837568 | bytes 10616832 | tf_op jit(solution)/shard_map/dot_general | solution.py:30
  (177 shorter events, 98.9 us)
Async XLA Ops:
  8.5 15.4 %collective-permute-start.1 = (bf16[128,768]{1,0:T(8,128)(2,1)S(1)}, bf16[128,768]{1,0:T(8,128)(2,1)S(1)}, u32[]{:S(2)}, u32[]{:S(2)}) collective-permute-start(bf16[128,768]{1,0:T(8,128)(2,1)S(1)} %bitcast.313), channel_id=1, source_target_pairs={{0,224},{16,240},{32,0},{48,16},{64,32},{80,48},{96,64},{112,80},{... | collective-permute-start | bytes 589832 | tf_op jit(solution)/shard_map/ppermute | solution.py:47
  14.5 21.1 %all-to-all-start = ((bf16[16,8,1536]{2,1,0:T(8,128)(2,1)}), bf16[16,8,1536]{2,1,0:T(8,128)(2,1)S(1)}, u32[]{:S(2)}, u32[]{:S(2)}) async-start(bf16[16,8,1536]{2,1,0:T(8,128)(2,1)} %bitcast.341), calls=%async_computation | async-start | bytes 786432 | tf_op jit(solution)/shard_map/all_to_all | solution.py:118
  20.3 267.3 %all-gather.2.cloned.1.call-start = ((), (), s32[]{:S(2)}) async-start(), calls=%async_computation.1 | async-start | bytes 3538944 | tf_op jit(solution)/shard_map/all_gather | solution.py:115
  20.4 12.9 %collective-permute-start = (bf16[1,128,768]{2,1,0:T(8,128)(2,1)S(1)}, bf16[1,128,768]{2,1,0:T(8,128)(2,1)}, u32[]{:S(2)}, u32[]{:S(2)}) collective-permute-start(bf16[1,128,768]{2,1,0:T(8,128)(2,1)S(1)} %bitcast.315), channel_id=1, source_target_pairs={{0,16},{16,0},{32,48},{48,32},{64,80},{80,64},{96,112},{112,96},{1... | collective-permute-start | bytes 589832 | tf_op jit(solution)/shard_map/ppermute | solution.py:51
  24.7 41.8 %collective-permute-start.3 = (bf16[2,128,768]{2,1,0:T(8,128)(2,1)}, bf16[2,128,768]{2,1,0:T(8,128)(2,1)}, u32[]{:S(2)}, u32[]{:S(2)}) collective-permute-start(bf16[2,128,768]{2,1,0:T(8,128)(2,1)} %pad_maximum_fusion.5), channel_id=1, source_target_pairs={{0,16},{16,0},{32,48},{48,32},{64,80},{80,64},{96,112},{112,96},{1... | collective-permute-start | bytes 1179656 | tf_op jit(solution)/shard_map/ppermute | solution.py:51
  40.1 15.2 %collective-permute-start.17 = (bf16[2,128,768]{2,1,0:T(8,128)(2,1)S(1)}, bf16[2,128,768]{2,1,0:T(8,128)(2,1)S(1)}, u32[]{:S(2)}, u32[]{:S(2)}) collective-permute-start(bf16[2,128,768]{2,1,0:T(8,128)(2,1)S(1)} %pad_maximum_fusion.6), channel_id=1, source_target_pairs={{0,16},{16,0},{32,48},{48,32},{64,80},{80,64},{96,112},{112,96},{1... | collective-permute-start | bytes 1179656 | tf_op jit(solution)/shard_map/ppermute | solution.py:51
  46.2 16.0 %collective-permute-start.20 = (bf16[2,128,768]{2,1,0:T(8,128)(2,1)S(1)}, bf16[2,128,768]{2,1,0:T(8,128)(2,1)S(1)}, u32[]{:S(2)}, u32[]{:S(2)}) collective-permute-start(bf16[2,128,768]{2,1,0:T(8,128)(2,1)S(1)} %pad_maximum_fusion.7), channel_id=1, source_target_pairs={{0,16},{16,0},{32,48},{48,32},{64,80},{80,64},{96,112},{112,96},{1... | collective-permute-start | bytes 1179656 | tf_op jit(solution)/shard_map/ppermute | solution.py:51
  52.6 11.7 %collective-permute-start.23 = (bf16[1,128,768]{2,1,0:T(8,128)(2,1)S(1)}, bf16[1,128,768]{2,1,0:T(8,128)(2,1)S(1)}, u32[]{:S(2)}, u32[]{:S(2)}) collective-permute-start(bf16[1,128,768]{2,1,0:T(8,128)(2,1)S(1)} %bitcast.339), channel_id=1, source_target_pairs={{0,16},{16,0},{32,48},{48,32},{64,80},{80,64},{96,112},{112,96},{1... | collective-permute-start | bytes 589832 | tf_op jit(solution)/shard_map/ppermute | solution.py:51
  72.3 15.7 %collective-permute-start.25 = (bf16[10,2,8,1536]{3,2,0,1:T(8,128)(2,1)S(1)}, bf16[10,2,8,1536]{3,2,0,1:T(8,128)(2,1)S(1)}, u32[]{:S(2)}, u32[]{:S(2)}) collective-permute-start(bf16[10,2,8,1536]{3,2,0,1:T(8,128)(2,1)S(1)} %bitcast.336), channel_id=1, source_target_pairs={{0,4},{1,5},{2,6},{3,7},{4,0},{5,1},{6,2},{7,3},{8,12},{9,13},{10,... | collective-permute-start | bytes 1474568 | tf_op jit(solution)/shard_map/ppermute | solution.py:61
  74.5 23.2 %collective-permute-start.26 = (bf16[10,2,8,1536]{3,2,0,1:T(8,128)(2,1)S(1)}, bf16[10,2,8,1536]{3,2,0,1:T(8,128)(2,1)S(1)}, u32[]{:S(2)}, u32[]{:S(2)}) collective-permute-start(bf16[10,2,8,1536]{3,2,0,1:T(8,128)(2,1)S(1)} %bitcast.337), channel_id=1, source_target_pairs={{0,2},{1,3},{2,4},{3,5},{4,6},{5,7},{6,0},{7,1},{8,10},{9,11},{10,... | collective-permute-start | bytes 1474568 | tf_op jit(solution)/shard_map/ppermute | solution.py:61
  74.6 23.1 %collective-permute-start.27 = (bf16[10,2,8,1536]{3,2,0,1:T(8,128)(2,1)S(1)}, bf16[10,2,8,1536]{3,2,0,1:T(8,128)(2,1)S(1)}, u32[]{:S(2)}, u32[]{:S(2)}) collective-permute-start(bf16[10,2,8,1536]{3,2,0,1:T(8,128)(2,1)S(1)} %bitcast.338), channel_id=1, source_target_pairs={{0,6},{1,7},{2,0},{3,1},{4,2},{5,3},{6,4},{7,5},{8,14},{9,15},{10,... | collective-permute-start | bytes 1474568 | tf_op jit(solution)/shard_map/ppermute | solution.py:61
  77.9 29.4 %collective-permute-start.4 = (bf16[6,64,1536]{2,1,0:T(8,128)(2,1)S(1)}, bf16[6,64,1536]{2,1,0:T(8,128)(2,1)S(1)}, u32[]{:S(2)}, u32[]{:S(2)}) collective-permute-start(bf16[6,64,1536]{2,1,0:T(8,128)(2,1)S(1)} %convolution_convert_fusion.2), channel_id=1, source_target_pairs={{0,1},{1,0},{2,3},{3,2},{4,5},{5,4},{6,7},{7,6},{8,9},{9,8},{10,11... | collective-permute-start | bytes 3538952 | tf_op jit(solution)/shard_map/ppermute | solution.py:69
  113.4 27.3 %collective-permute-start.30 = (bf16[10,2,8,1536]{3,2,0,1:T(8,128)(2,1)S(1)}, bf16[10,2,8,1536]{3,2,0,1:T(8,128)(2,1)S(1)}, u32[]{:S(2)}, u32[]{:S(2)}) collective-permute-start(bf16[10,2,8,1536]{3,2,0,1:T(8,128)(2,1)S(1)} %get-tuple-element.22), channel_id=1, source_target_pairs={{0,6},{1,7},{2,0},{3,1},{4,2},{5,3},{6,4},{7,5},{8,14},{9,15},{10,... | collective-permute-start | bytes 1474568 | tf_op jit(solution)/shard_map/ppermute | solution.py:61
  114.2 28.1 %collective-permute-start.31 = (bf16[10,2,8,1536]{3,2,0,1:T(8,128)(2,1)S(1)}, bf16[10,2,8,1536]{3,2,0,1:T(8,128)(2,1)S(1)}, u32[]{:S(2)}, u32[]{:S(2)}) collective-permute-start(bf16[10,2,8,1536]{3,2,0,1:T(8,128)(2,1)S(1)} %get-tuple-element.22), channel_id=1, source_target_pairs={{0,4},{1,5},{2,6},{3,7},{4,0},{5,1},{6,2},{7,3},{8,12},{9,13},{10,... | collective-permute-start | bytes 1474568 | tf_op jit(solution)/shard_map/ppermute | solution.py:61
  115.7 26.5 %collective-permute-start.32 = (bf16[10,2,8,1536]{3,2,0,1:T(8,128)(2,1)S(1)}, bf16[10,2,8,1536]{3,2,0,1:T(8,128)(2,1)S(1)}, u32[]{:S(2)}, u32[]{:S(2)}) collective-permute-start(bf16[10,2,8,1536]{3,2,0,1:T(8,128)(2,1)S(1)} %get-tuple-element.22), channel_id=1, source_target_pairs={{0,2},{1,3},{2,4},{3,5},{4,6},{5,7},{6,0},{7,1},{8,10},{9,11},{10,... | collective-permute-start | bytes 1474568 | tf_op jit(solution)/shard_map/ppermute | solution.py:61
  118.4 33.2 %collective-permute-start.5 = (bf16[6,2,8,1536]{3,2,0,1:T(8,128)(2,1)S(1)}, bf16[6,2,8,1536]{3,2,0,1:T(8,128)(2,1)S(1)}, u32[]{:S(2)}, u32[]{:S(2)}) collective-permute-start(bf16[6,2,8,1536]{3,2,0,1:T(8,128)(2,1)S(1)} %bitcast.345), channel_id=1, source_target_pairs={{0,4},{1,5},{2,6},{3,7},{4,0},{5,1},{6,2},{7,3},{8,12},{9,13},{10,... | collective-permute-start | bytes 884744 | tf_op jit(solution)/shard_map/ppermute | solution.py:61
  119.9 31.7 %collective-permute-start.6 = (bf16[6,2,8,1536]{3,2,0,1:T(8,128)(2,1)S(1)}, bf16[6,2,8,1536]{3,2,0,1:T(8,128)(2,1)S(1)}, u32[]{:S(2)}, u32[]{:S(2)}) collective-permute-start(bf16[6,2,8,1536]{3,2,0,1:T(8,128)(2,1)S(1)} %bitcast.346), channel_id=1, source_target_pairs={{0,2},{1,3},{2,4},{3,5},{4,6},{5,7},{6,0},{7,1},{8,10},{9,11},{10,... | collective-permute-start | bytes 884744 | tf_op jit(solution)/shard_map/ppermute | solution.py:61
  142.6 27.1 %collective-permute-start.33 = (bf16[10,2,4,8,1536]{4,3,0,1,2:T(8,128)(2,1)S(1)}, bf16[10,2,4,8,1536]{4,3,0,1,2:T(8,128)(2,1)S(1)}, u32[]{:S(2)}, u32[]{:S(2)}) collective-permute-start(bf16[10,2,4,8,1536]{4,3,0,1,2:T(8,128)(2,1)S(1)} %get-tuple-element.8), channel_id=1, source_target_pairs={{0,1},{1,0},{2,3},{3,2},{4,5},{5,4},{6,7},{7,6},{8,9},{9,8},{10,11... | collective-permute-start | bytes 5898248 | tf_op jit(solution)/shard_map/ppermute | solution.py:69
  163.9 14.2 %collective-permute-start.10 = (bf16[6,2,8,1536]{3,2,1,0:T(8,128)(2,1)S(1)}, bf16[6,2,8,1536]{3,2,1,0:T(8,128)(2,1)S(1)}, u32[]{:S(2)}, u32[]{:S(2)}) collective-permute-start(bf16[6,2,8,1536]{3,2,1,0:T(8,128)(2,1)S(1)} %get-tuple-element.33), channel_id=1, source_target_pairs={{0,6},{1,7},{2,0},{3,1},{4,2},{5,3},{6,4},{7,5},{8,14},{9,15},{10,... | collective-permute-start | bytes 884744 | tf_op jit(solution)/shard_map/ppermute | solution.py:61
  168.2 11.6 %collective-permute-start.11 = (bf16[6,2,8,1536]{3,2,1,0:T(8,128)(2,1)S(1)}, bf16[6,2,8,1536]{3,2,1,0:T(8,128)(2,1)S(1)}, u32[]{:S(2)}, u32[]{:S(2)}) collective-permute-start(bf16[6,2,8,1536]{3,2,1,0:T(8,128)(2,1)S(1)} %get-tuple-element.33), channel_id=1, source_target_pairs={{0,4},{1,5},{2,6},{3,7},{4,0},{5,1},{6,2},{7,3},{8,12},{9,13},{10,... | collective-permute-start | bytes 884744 | tf_op jit(solution)/shard_map/ppermute | solution.py:61
  168.2 12.4 %collective-permute-start.12 = (bf16[6,2,8,1536]{3,2,1,0:T(8,128)(2,1)S(1)}, bf16[6,2,8,1536]{3,2,1,0:T(8,128)(2,1)S(1)}, u32[]{:S(2)}, u32[]{:S(2)}) collective-permute-start(bf16[6,2,8,1536]{3,2,1,0:T(8,128)(2,1)S(1)} %get-tuple-element.33), channel_id=1, source_target_pairs={{0,2},{1,3},{2,4},{3,5},{4,6},{5,7},{6,0},{7,1},{8,10},{9,11},{10,... | collective-permute-start | bytes 884744 | tf_op jit(solution)/shard_map/ppermute | solution.py:61
  175.5 23.5 %collective-permute-start.34 = (bf16[5,128,768]{2,1,0:T(8,128)(2,1)S(1)}, bf16[5,128,768]{2,1,0:T(8,128)(2,1)S(1)}, u32[]{:S(2)}, u32[]{:S(2)}) collective-permute-start(bf16[5,128,768]{2,1,0:T(8,128)(2,1)S(1)} %slice_bitcast_fusion), channel_id=1, source_target_pairs={{0,16},{16,0},{32,48},{48,32},{64,80},{80,64},{96,112},{112,96},{1... | collective-permute-start | bytes 2949128 | tf_op jit(solution)/shard_map/ppermute | solution.py:51
  180.8 18.3 %collective-permute-start.13 = (bf16[6,2,4,8,1536]{4,3,2,1,0:T(8,128)(2,1)S(1)}, bf16[6,2,4,8,1536]{4,3,2,1,0:T(8,128)(2,1)S(1)}, u32[]{:S(2)}, u32[]{:S(2)}) collective-permute-start(bf16[6,2,4,8,1536]{4,3,2,1,0:T(8,128)(2,1)S(1)} %get-tuple-element.16), channel_id=1, source_target_pairs={{0,1},{1,0},{2,3},{3,2},{4,5},{5,4},{6,7},{7,6},{8,9},{9,8},{10,11... | collective-permute-start | bytes 3538952 | tf_op jit(solution)/shard_map/ppermute | solution.py:69
  214.0 11.7 %collective-permute-start.14 = (bf16[3,128,768]{2,1,0:T(8,128)(2,1)S(1)}, bf16[3,128,768]{2,1,0:T(8,128)(2,1)S(1)}, u32[]{:S(2)}, u32[]{:S(2)}) collective-permute-start(bf16[3,128,768]{2,1,0:T(8,128)(2,1)S(1)} %slice_bitcast_fusion.5), channel_id=1, source_target_pairs={{0,16},{16,0},{32,48},{48,32},{64,80},{80,64},{96,112},{112,96},{1... | collective-permute-start | bytes 1769480 | tf_op jit(solution)/shard_map/ppermute | solution.py:51
  (31 other events, 271.6 us)
Sparse Core Ops, SparseCore 0:
  243.9 43.6 all-gather.1
